TPU v7x, 32 devices: a whole 2x2x4 slice. The times are simulated.
32 devices in a mesh: seq: 8 (over z, x), head: 4 (over y, core).
Axes of the slice: x: 2, y: 2, z: 4, core: 2. Of those that a mesh axis runs over, the one named last changes fastest.
Arguments:
- tokens: bfloat16 [2048, 1536], P('seq'), may hold values from -6 to 6
- attn_gain: float32 [1536], replicated, may hold values from 0.5 to 1.5
- query_weight: bfloat16 [1536, 1536], P('seq', 'head'), may hold values from -0.15625 to 0.15625
- key_weight: bfloat16 [1536, 1536], P('seq', 'head'), may hold values from -0.15625 to 0.15625
- value_weight: bfloat16 [1536, 1536], P('seq', 'head'), may hold values from -0.15625 to 0.15625
- forget_weight: bfloat16 [1536, 24], P('seq', 'head'), may hold values from -0.15625 to 0.15625
- forget_bias: float32 [24], P('head'), may hold values from 3 to 10
- out_weight: bfloat16 [1536, 1536], P('head', 'seq'), may hold values from -1.5 to 1.5
- ffn_gain: float32 [1536], replicated, may hold values from 0.5 to 1.5
- gate_weight: bfloat16 [1536, 4096], P('seq', 'head'), may hold values from -0.15625 to 0.15625
- up_weight: bfloat16 [1536, 4096], P('seq', 'head'), may hold values from -0.15625 to 0.15625
- down_weight: bfloat16 [4096, 1536], P('head', 'seq'), may hold values from -0.09375 to 0.09375
- doc_lengths: int32 [4], replicated, may hold values from 1 to 1024, 2048 in all
- out_grad: bfloat16 [2048, 1536], P('seq'), may hold values from -6 to 6
Outputs:
- layer_out: bfloat16 [2048, 1536], P('seq')
- tokens_grad: bfloat16 [2048, 1536], P('seq')
- attn_gain_grad: float32 [1536], replicated
- query_weight_grad: float32 [1536, 1536], P('seq', 'head')
- key_weight_grad: float32 [1536, 1536], P('seq', 'head')
- value_weight_grad: float32 [1536, 1536], P('seq', 'head')
- forget_weight_grad: float32 [1536, 24], P('seq', 'head')
- forget_bias_grad: float32 [24], P('head')
- out_weight_grad: float32 [1536, 1536], P('head', 'seq')
- ffn_gain_grad: float32 [1536], replicated
- gate_weight_grad: float32 [1536, 4096], P('seq', 'head')
- up_weight_grad: float32 [1536, 4096], P('seq', 'head')
- down_weight_grad: float32 [4096, 1536], P('head', 'seq')
Inputs may be any that keep to these rules, and one draw needn't show every extreme that they name: `doc_lengths`: document lengths in position order summing to 2048; the longest is exactly 1024.
All inputs are finite; a program needn't handle non-finite values.
Results may differ from a plain program's by a relative error of at most 0.02.
Values may be sent and summed in bfloat16 or wider, within the bound.
A program may use at most 256 MiB of HBM per device.

v0:
```python
import jax
import jax.numpy as jnp
from jax import lax
from jax.experimental import pallas as pl
from jax.experimental.pallas import tpu as pltpu
from jax.sharding import PartitionSpec as P

HEAD_DIM = 64
EPSILON = 1e-06
HIGHEST = lax.Precision.HIGHEST
MASKED = -1e30
MESH_ID = pl.DeviceIdType.MESH
F32 = jnp.float32
BF16 = jnp.bfloat16
LANES = 128
KEY_TILES = ((0, 0), (0, 1), (1, 0))
VALUE_TILES = ((1, 1), (2, 0), (2, 1))
OUT_TILES = ((0, 1), (1, 0), (1, 1))
NEAR_FIRST = (1, 3, 2)


def dot_nn(left, right):
    return jnp.dot(left, right, preferred_element_type=F32)


def dot_nt(left, right):
    return lax.dot_general(left, right, (((1,), (1,)), ((), ())), preferred_element_type=F32)


def dot_tn(left, right):
    return lax.dot_general(left, right, (((0,), (0,)), ((), ())), preferred_element_type=F32)


def rows_of(first, count):
    return pl.ds(pl.multiple_of(first, 16), count)


def add_to(ref, other):
    ref[...] = (ref[...].astype(F32) + other[...].astype(F32)).astype(BF16)


class Net:
    def __init__(self, sems):
        s = lax.axis_index("seq")
        h = lax.axis_index("head")
        self.line = 4
        self.z, self.x = s // 2, s % 2
        self.y, self.c = h // 2, h % 2
        self.inner = (self.z == 1) | (self.z == 2)
        self.group = self.z * 2 + self.y
        self.sems = sems
        self.used = 0
        self.pending = []

    def alloc(self, count):
        first = self.used
        self.used += count
        return first

    def to(self, z=None, x=None, y=None, c=None):
        z = self.z if z is None else z
        x = self.x if x is None else x
        y = self.y if y is None else y
        c = self.c if c is None else c
        return (z * 2 + x, y * 2 + c)

    def by_distance(self):
        low = self.z < 2
        nearest = self.z + 1 - 2 * (self.z % 2)
        return (nearest, jnp.where(low, 2, 1), jnp.where(low, 3, 0))

    def side(self):
        return self.to(x=1 - self.x)

    def lower(self):
        return self.to(c=1 - self.c)

    def upper(self):
        return self.to(y=1 - self.y)

    def next(self, step):
        return (self.z + step) % self.line

    def announce(self):
        sem = pltpu.get_barrier_semaphore()
        peers = [self.side(), self.lower(), self.upper()]
        peers.append(self.to(x=1 - self.x, c=1 - self.c))
        peers.append(self.to(y=1 - self.y, c=1 - self.c))
        for step in range(1, self.line):
            z = self.next(step)
            peers += [self.to(z=z), self.to(z=z, c=1 - self.c)]
            peers += [self.to(z=z, x=1 - self.x), self.to(z=z, y=1 - self.y)]
        for peer in peers:
            pl.semaphore_signal(sem, 1, device_id=peer, device_id_type=MESH_ID)
        self.peers = len(peers)

    def await_peers(self):
        pl.semaphore_wait(pltpu.get_barrier_semaphore(), self.peers)

    def copy(self, src, dst, send, recv, device):
        return pltpu.make_async_remote_copy(
            src_ref=src,
            dst_ref=dst,
            send_sem=self.sems.at[send],
            recv_sem=self.sems.at[recv],
            device_id=device,
            device_id_type=MESH_ID,
        )

    def begin(self, made):
        made.start()
        self.pending.append(made.wait_send)
        return made

    def begin_if(self, condition, made):
        pl.when(condition)(made.start)
        self.pending.append(lambda: pl.when(condition)(made.wait_send))

    def send(self, src, dst, device):
        first = self.alloc(2)
        return self.begin(self.copy(src, dst, first, first + 1, device))

    def got(self, ref, recv):
        self.copy(ref, ref, recv, recv, self.side()).wait_recv()

    def drain(self):
        for wait in self.pending:
            wait()
        self.pending = []


class RowGather:
    def __init__(self, net, slot, lower=None):
        self.net = net
        self.slot = slot
        self.low = lower
        self.sent = net.alloc(4)
        self.came = net.alloc(4)
        self.up_sent = net.alloc(4)
        self.up_came = net.alloc(4)
        self.low_sent = net.alloc(8)
        self.low_came = net.alloc(8)

    def pass_low(self, y, z):
        if self.low is not None:
            net = self.net
            index = y * 4 + z
            block = self.slot(y, z)
            net.begin(
                net.copy(
                    block, block, self.low_sent + index, self.low_came + index, net.lower()
                )
            )

    def pass_up(self, z):
        net = self.net
        block = self.slot(net.y, z)
        net.begin(net.copy(block, block, self.up_sent + z, self.up_came + z, net.upper()))
        self.pass_low(net.y, z)

    def along(self, src, to):
        net = self.net
        block = self.slot(net.y, src)
        return net.copy(block, block, self.sent + to, self.came + src, net.to(z=to))

    def start(self):
        net = self.net
        for to in range(net.line):
            gap = jnp.abs(to - net.z)
            net.begin_if((gap > 0) & (gap < 3), self.along(net.z, to))
        self.pass_up(net.z)

    def forward(self):
        net = self.net
        for src in net.by_distance():
            net.got(self.slot(net.y, src), self.came + src)
            self.pass_up(src)
        far = net.by_distance()[2]
        net.begin_if(net.inner, self.along(far, 3 - far))

    def finish(self):
        net = self.net
        for src in (net.z,) + net.by_distance():
            net.got(self.slot(1 - net.y, src), self.up_came + src)
            self.pass_low(1 - net.y, src)
        if self.low is not None:
            for y in range(2):
                for z in range(4):
                    net.got(self.low(y, z), self.low_came + y * 4 + z)


class RowSum:
    def __init__(self, net, slot, recv_up, recv_line):
        self.net = net
        self.slot = slot
        self.recv_up = recv_up
        self.recv_line = recv_line
        self.up_sent = net.alloc(4)
        self.up_came = net.alloc(4)
        self.sent = net.alloc(4)
        self.came = net.alloc(4)

    def start(self):
        net = self.net
        for z in net.by_distance()[::-1] + (net.z,):
            net.begin(
                net.copy(
                    self.slot(1 - net.y, z),
                    self.recv_up(z),
                    self.up_sent + z,
                    self.up_came + z,
                    net.upper(),
                )
            )

    def add_up(self, z):
        self.net.got(self.recv_up(z), self.up_came + z)
        add_to(self.slot(self.net.y, z), self.recv_up(z))

    def along(self, target, hop, place):
        net = self.net
        return net.copy(
            self.slot(net.y, target),
            self.recv_line(place),
            self.sent + target,
            self.came + place,
            net.to(z=hop),
        )

    def middle(self):
        net = self.net
        nearest, other, far = net.by_distance()
        self.add_up(far)
        net.begin_if(jnp.logical_not(net.inner), self.along(far, nearest, nearest))
        for z in (other, nearest):
            self.add_up(z)
            net.begin(self.along(z, z, net.z))

        @pl.when(net.inner)
        def _():
            net.got(self.recv_line(net.z), self.came + net.z)
            add_to(self.slot(net.y, far), self.recv_line(net.z))

        net.begin_if(net.inner, self.along(far, far, net.z))
        self.add_up(net.z)

    def result(self):
        net = self.net
        nearest, other, far = net.by_distance()

        @pl.when(jnp.logical_not(net.inner))
        def _():
            self.recv_line(far)[...] = jnp.zeros_like(self.recv_line(far))

        total = self.slot(net.y, net.z)[...].astype(F32)
        for z in (nearest, other):
            net.got(self.recv_line(z), self.came + z)
            total = total + self.recv_line(z)[...].astype(F32)
        pl.when(net.inner)(lambda: net.got(self.recv_line(far), self.came + far))
        return total + self.recv_line(far)[...].astype(F32)


class CrossGather:
    def __init__(self, net, slot):
        self.net = net
        self.slot = slot

    def start(self):
        net = self.net
        mine = self.slot(net.x, net.c)
        self.across = net.send(mine, mine, net.side())
        self.low = net.send(mine, mine, net.lower())

    def forward(self):
        net = self.net
        self.across.wait_recv()
        other = self.slot(1 - net.x, net.c)
        self.both = net.send(other, other, net.lower())

    def finish(self):
        self.low.wait_recv()
        self.both.wait_recv()


class Direct:
    def __init__(self, net, me, peers):
        self.net = net
        self.me = me
        self.peers = peers
        self.sent = net.alloc(8)
        self.came = net.alloc(8)

    def start(self, made, slot):
        net = self.net
        for at, (index, device) in enumerate(self.peers):
            net.begin(
                net.copy(
                    made(index), slot(self.me), self.sent + at, self.came + self.me, device
                )
            )

    def finish(self, slot):
        for index, _ in self.peers:
            self.net.got(slot(index), self.came + index)


class WeightSpread:
    def __init__(self, net, stage, full):
        self.net = net
        self.stage = stage
        self.full = full
        self.block = stage.shape[1]
        self.sent = net.alloc(2)
        self.came = net.alloc(4)
        self.side_sent = net.alloc(4)
        self.side_came = net.alloc(4)
        self.low_sent = net.alloc(8)
        self.low_came = net.alloc(8)
        self.first = (net.z // 2) == net.c

    def slot(self, z, x):
        return self.full.at[rows_of((z * 2 + x) * self.block, self.block), :]

    def away(self, u):
        net = self.net
        return net.copy(
            self.stage.at[u],
            self.slot(net.z, net.x),
            self.sent + u,
            self.came + net.z,
            net.to(z=2 * net.c + u),
        )

    def across(self, z):
        net = self.net
        block = self.slot(z, net.x)
        return net.copy(block, block, self.side_sent + z, self.side_came + z, net.side())

    def low(self, z, x):
        block = self.slot(z, x)
        index = z * 2 + x
        return self.net.copy(
            block, block, self.low_sent + index, self.low_came + index, self.net.lower()
        )

    def start(self):
        net = self.net
        for u in range(2):
            pl.when(2 * net.c + u != net.z)(lambda u=u: self.away(u).start())

        @pl.when(self.first)
        def _():
            self.slot(net.z, net.x)[...] = self.stage[net.z % 2]
            self.across(net.z).start()
            self.low(net.z, net.x).start()

    def forward(self):
        net = self.net

        @pl.when(self.first)
        def _():
            for step in NEAR_FIRST:
                src = net.next(step)
                net.got(self.slot(src, net.x), self.came + src)
                self.across(src).start()
                self.low(src, net.x).start()

    def finish(self):
        net = self.net

        @pl.when(self.first)
        def _():
            for step in (0,) + NEAR_FIRST:
                src = net.next(step)
                net.got(self.slot(src, 1 - net.x), self.side_came + src)
                self.low(src, 1 - net.x).start()

        @pl.when(jnp.logical_not(self.first))
        def _():
            for z in range(4):
                for x in range(2):
                    net.got(self.slot(z, x), self.low_came + z * 2 + x)

    def drain(self):
        net = self.net
        for u in range(2):
            pl.when(2 * net.c + u != net.z)(lambda u=u: self.away(u).wait_send())

        @pl.when(self.first)
        def _():
            for z in range(4):
                self.across(z).wait_send()
                for x in range(2):
                    self.low(z, x).wait_send()


class HiddenSpread:
    def __init__(self, net, stage, full):
        self.net = net
        self.stage = stage
        self.full = full
        self.block = stage.shape[1]
        self.sent = net.alloc(4)
        self.came = net.alloc(4)
        self.side_sent = net.alloc(4)
        self.side_came = net.alloc(4)

    def slot(self, z, x):
        return self.full.at[rows_of((z * 2 + x) * self.block, self.block), :]

    def across(self, z):
        net = self.net
        block = self.slot(z, net.x)
        net.begin(net.copy(block, block, self.side_sent + z, self.side_came + z, net.side()))

    def start(self):
        net = self.net
        self.slot(net.z, net.x)[...] = self.stage[net.z]
        for step in NEAR_FIRST:
            to = net.next(step)
            net.begin(
                net.copy(
                    self.stage.at[to],
                    self.slot(net.z, net.x),
                    self.sent + step,
                    self.came + net.z,
                    net.to(z=to),
                )
            )
        self.across(net.z)

    def forward(self):
        net = self.net
        for step in NEAR_FIRST:
            src = net.next(step)
            net.got(self.slot(src, net.x), self.came + src)
            self.across(src)

    def finish(self):
        net = self.net
        for z in range(4):
            net.got(self.slot(z, 1 - net.x), self.side_came + z)


class WeightSum:
    def __init__(self, net, grads, recv_low, recv_side, final):
        self.net = net
        self.grads = grads
        self.recv_low = recv_low
        self.recv_side = recv_side
        self.final = final
        self.block = final.shape[1]
        self.side_sent = net.alloc(2)
        self.side_came = net.alloc(2)
        self.sent = net.alloc(2)
        self.came = net.alloc(2)

    def rows(self, z, x):
        return self.grads.at[rows_of((z * 2 + x) * self.block, self.block), :]

    def start(self):
        net = self.net
        half = 4 * self.block
        self.low = net.send(
            self.grads.at[rows_of((1 - net.c) * half, half), :], self.recv_low, net.lower()
        )

    def second(self):
        net = self.net
        self.low.wait_recv()
        for x in (1 - net.x, net.x):
            for i in range(2):
                z = 2 * net.c + i
                add_to(
                    self.rows(z, x), self.recv_low.at[rows_of((i * 2 + x) * self.block, self.block)]
                )
        for i in range(2):
            net.begin(
                net.copy(
                    self.rows(2 * net.c + i, 1 - net.x),
                    self.recv_side.at[i],
                    self.side_sent + i,
                    self.side_came + i,
                    net.side(),
                )
            )

    def owner(self, i):
        net = self.net
        z = 2 * net.c + i
        made = net.copy(
            self.rows(z, net.x),
            self.final.at[net.z % 2],
            self.sent + i,
            self.came + net.z % 2,
            net.to(z=z, c=net.z // 2),
        )
        return (z == net.z) & (net.z // 2 == net.c), made

    def third(self):
        net = self.net
        for i in range(2):
            net.got(self.recv_side.at[i], self.side_came + i)
            mine = self.rows(2 * net.c + i, net.x)
            add_to(mine, self.recv_side.at[i])
            local, made = self.owner(i)

            @pl.when(local)
            def _():
                self.final[net.z % 2] = mine[...]

            pl.when(jnp.logical_not(local))(made.start)

    def finish(self):
        net = self.net
        for u in range(2):
            pl.when(2 * net.c + u != net.z)(
                lambda u=u: net.got(self.final.at[u], self.came + u)
            )

    def drain(self):
        for i in range(2):
            local, made = self.owner(i)
            pl.when(jnp.logical_not(local))(made.wait_send)


class HiddenSum:
    def __init__(self, net, grads, recv_side, final):
        self.net = net
        self.grads = grads
        self.recv_side = recv_side
        self.final = final
        self.block = final.shape[1]
        self.side_sent = net.alloc(4)
        self.side_came = net.alloc(4)
        self.sent = net.alloc(4)
        self.came = net.alloc(4)

    def rows(self, z, x):
        return self.grads.at[rows_of((z * 2 + x) * self.block, self.block), :]

    def start(self):
        net = self.net
        for step in (2, 1, 3, 0):
            z = net.next(step)
            net.begin(
                net.copy(
                    self.rows(z, 1 - net.x),
                    self.recv_side.at[z],
                    self.side_sent + z,
                    self.side_came + z,
                    net.side(),
                )
            )

    def second(self):
        net = self.net
        for step in (2, 1, 3, 0):
            z = net.next(step)
            net.got(self.recv_side.at[z], self.side_came + z)
            mine = self.rows(z, net.x)
            add_to(mine, self.recv_side.at[z])
            if step:
                net.begin(
                    net.copy(
                        mine,
                        self.final.at[net.z],
                        self.sent + step,
                        self.came + net.z,
                        net.to(z=z),
                    )
                )
            else:
                self.final[net.z] = mine[...]

    def finish(self):
        net = self.net
        for step in NEAR_FIRST:
            src = net.next(step)
            net.got(self.final.at[src], self.came + src)


class Places:
    def __init__(self, net, chunk):
        self.net = net
        self.chunk = chunk
        self.part = 4 * chunk
        self.all = 32 * chunk

    def position(self, at):
        chunk = self.chunk
        late = at // (16 * chunk)
        x = (at // (8 * chunk)) % 2
        c = (at // (4 * chunk)) % 2
        z = (at // chunk) % 4
        owner = 2 * z + x
        group = jnp.where(late == 0, owner, 15 - owner)
        return group * (2 * chunk) + c * chunk + at % chunk

    def own(self, late):
        return (late * 4 + self.net.x * 2 + self.net.c) * self.part

    def every(self, shape, axis):
        return self.position(lax.broadcasted_iota(jnp.int32, shape, axis))


def doc_starts(positions, doc_ref):
    start = jnp.zeros(positions.shape, jnp.int32)
    end = jnp.int32(0)
    for k in range(doc_ref.shape[0] - 1):
        end = end + doc_ref[k]
        start = jnp.where(positions >= end, end, start)
    return start


def running_sums(places, rows_in, spread, gather):
    tiles = places.all // LANES
    chunk = places.chunk
    row = lax.broadcasted_iota(jnp.int32, (LANES, LANES), 0)
    col = lax.broadcasted_iota(jnp.int32, (LANES, LANES), 1)
    within = ((row // chunk == col // chunk) & (row <= col)).astype(F32)
    stacked = jnp.concatenate(
        [rows_in[:, k * LANES : (k + 1) * LANES] for k in range(tiles)], axis=0
    )
    inside = jnp.dot(stacked, within, precision=HIGHEST, preferred_element_type=F32)
    outside = jnp.dot(rows_in, spread[...], precision=HIGHEST, preferred_element_type=F32)
    outside = outside[:, : gather.shape[0]]
    outside = jnp.dot(outside, gather[...], precision=HIGHEST, preferred_element_type=F32)
    return outside + jnp.concatenate(
        [inside[k * 8 : (k + 1) * 8, :] for k in range(tiles)], axis=1
    )


def order_tables(places, spread, gather):
    order = places.every((places.all, LANES), 0) // places.chunk
    slot = lax.broadcasted_iota(jnp.int32, (places.all, LANES), 1)
    spread[...] = (order < slot).astype(F32)
    order = places.every(gather.shape, 1) // places.chunk
    slot = lax.broadcasted_iota(jnp.int32, gather.shape, 0)
    gather[...] = (order == slot).astype(F32)


def tile_of(ref, rows, tile):
    return ref[rows, tile * LANES : (tile + 1) * LANES]


def only(values_in, lane, side):
    return jnp.where(lane // HEAD_DIM == side, values_in, jnp.zeros_like(values_in))


def norm_grad(grad_in, values_in, gain):
    inverse = lax.rsqrt(jnp.mean(values_in * values_in, axis=-1, keepdims=True) + EPSILON)
    normed = values_in * inverse
    scaled = grad_in * gain
    inner = jnp.mean(scaled * normed, axis=-1, keepdims=True)
    return inverse * (scaled - normed * inner), jnp.sum(grad_in * normed, axis=0, keepdims=True)


def norm(values_in, gain):
    inverse = lax.rsqrt(jnp.mean(values_in * values_in, axis=-1, keepdims=True) + EPSILON)
    return (values_in * inverse * gain).astype(BF16)


def to_columns(rows_in, first=0):
    many = rows_in.shape[1]
    parts = [rows_in, jnp.zeros((LANES - 8 - first, many), F32)]
    if first:
        parts = [jnp.zeros((first, many), F32)] + parts
    return jnp.concatenate(parts, axis=0).T


def gather_quarters(net, ref):
    chunk = ref.shape[0] // 4

    def piece(y):
        return ref.at[rows_of((2 * y + net.c) * chunk, chunk), :]

    up = net.send(piece(net.y), piece(net.y), net.upper())
    first = net.send(piece(net.y), piece(net.y), net.lower())

    def second():
        up.wait_recv()
        other = net.send(piece(1 - net.y), piece(1 - net.y), net.lower())

        def last():
            first.wait_recv()
            other.wait_recv()

        return last

    return second


def layer_kernel(
    tokens,
    out_grad,
    gain_one,
    gain_two,
    wq,
    wk,
    wv,
    forget_t,
    bias_in,
    wo_t,
    wg,
    wu,
    wd_t,
    doc_ref,
    layer_out,
    tokens_grad,
    gains,
    bias_grad,
    late_final,
    last_final,
    early_final,
    ffn_final,
    stage_attn,
    stage_out,
    stage_bias,
    other_bias,
    h_one,
    allowed,
    spread,
    gather,
    logit_parts,
    queries,
    keyval,
    offsets,
    mass,
    logits,
    mixed,
    exact,
    middle,
    normed_two,
    out_grads,
    w_attn,
    w_out,
    w_ffn,
    all_query,
    all_grad,
    ffn_grads,
    part_two,
    part_out,
    two_low,
    two_up,
    two_line,
    out_low,
    out_up,
    out_line,
    ffn_sum,
    ffn_side,
    late_sum,
    late_low,
    late_side,
    last_sum,
    last_low,
    last_side,
    early_sum,
    early_low,
    early_side,
    grad_attn,
    grad_heads,
    stats,
    off_parts,
    every_off,
    grad_qkv,
    grad_offs,
    part_one,
    one_up,
    one_line,
    gain_parts,
    gain_swap,
    own_tokens,
    all_forget,
    own_logits,
    near_sems,
    sems,
):
    net = Net(sems)
    net.announce()
    z, x, y, c = net.z, net.x, net.y, net.c
    width = tokens.shape[1]
    chunk = tokens.shape[0] // 4
    part = 4 * chunk
    places = Places(net, chunk)
    hidden = wg.shape[1] // 4
    own = rows_of((2 * y + c) * chunk, chunk)
    tile = 256
    scale_one = gain_one[...].reshape(1, width)
    scale_two = gain_two[...].reshape(1, width)

    token_net = RowGather(net, lambda yy, zz: grad_attn.at[yy, rows_of(zz * chunk, chunk), :])
    weight_net = WeightSpread(net, stage_attn, w_attn)
    out_net = WeightSpread(net, stage_out, w_out)
    units_net = HiddenSpread(net, ffn_side, w_ffn)
    kv_nets = [
        CrossGather(net, lambda xx, cc, late=late: keyval.at[late, xx, cc]) for late in range(2)
    ]
    sub = chunk // 2
    pieces = [slice(0, sub), slice(sub, chunk)]

    def piece_of(ref, k):
        return lambda zz: ref.at[zz, pieces[k], :]

    def rows_at(ref, k):
        return lambda yy, zz: ref.at[yy, rows_of(zz * chunk + k * sub, sub), :]

    logit_net = CrossGather(net, lambda xx, cc: logit_parts.at[xx, cc])
    two_nets = [
        RowGather(
            net,
            lambda yy, zz, k=k: normed_two.at[c, yy, zz, pieces[k], :],
            lambda yy, zz, k=k: normed_two.at[1 - c, yy, zz, pieces[k], :],
        )
        for k in range(2)
    ]
    given_net = RowGather(
        net, lambda yy, zz: out_grads.at[c, yy, zz], lambda yy, zz: out_grads.at[1 - c, yy, zz]
    )
    attn_sums = [
        RowSum(net, rows_at(part_one, k), piece_of(one_up, k), piece_of(one_line, k))
        for k in range(2)
    ]

    def groups():
        found = [(z * 2 + 1 - y, net.upper())]
        for step in range(1, 4):
            far = net.next(step)
            found.append((far * 2 + y, net.to(z=far)))
            found.append((far * 2 + 1 - y, net.to(z=far, y=1 - y)))
        return found

    forget_net = Direct(net, net.group, groups())
    logit_back = Direct(net, net.group, groups())
    rest = [(z * 2 + 1 - x, net.side())]
    for step in range(1, 4):
        far = net.next(step)
        rest.append((far * 2 + x, net.to(z=far)))
        rest.append((far * 2 + 1 - x, net.to(z=far, x=1 - x)))
    gain_net = Direct(net, z * 2 + x, rest)
    corner = net.to(y=1 - y, c=1 - c)
    last_gain = Direct(
        net,
        y * 2 + c,
        [(y * 2 + 1 - c, net.lower()), (2 - 2 * y + c, net.upper()), (3 - 2 * y - c, corner)],
    )

    near = [
        (tokens.at[own, :], own_tokens),
        (tokens.at[own, :], grad_attn.at[y, rows_of(z * chunk, chunk), :]),
        (out_grad.at[own, :], out_grads.at[c, y, z]),
    ]
    for index, ref in enumerate((wg, wu, wd_t)):
        for zz in range(4):
            near.append(
                (
                    ref.at[:, zz * hidden : (zz + 1) * hidden],
                    ffn_side.at[zz, :, index * hidden : (index + 1) * hidden],
                )
            )
    fetched = [
        pltpu.make_async_copy(src, dst, near_sems.at[at]) for at, (src, dst) in enumerate(near)
    ]
    for copy in fetched:
        copy.start()
    half_cols = wq.shape[1] // 2
    half_heads = half_cols // HEAD_DIM
    block = wq.shape[0]
    forget = forget_t[...].astype(F32)
    row8 = lax.broadcasted_iota(jnp.int32, (8, LANES), 0)
    for u in range(2):
        cols = slice(u * half_cols, (u + 1) * half_cols)
        for index, ref in enumerate((wk, wv)):
            stage_attn[u, :, index * half_cols : (index + 1) * half_cols] = ref[:, cols]
        rows8 = jnp.concatenate(
            [
                forget[u * half_heads : (u + 1) * half_heads, :],
                jnp.zeros((8 - half_heads, block), F32),
            ],
            axis=0,
        )
        rows8 = jnp.concatenate([rows8, jnp.zeros((8, 2 * LANES - block), F32)], axis=1)
        stage_attn[u, :, 4 * LANES :] = to_columns(rows8, HEAD_DIM)[:block].astype(BF16)
        stage_attn[u, :, 2 * half_cols : 3 * half_cols] = wq[:, cols]
        biases = jnp.zeros((8, LANES), F32)
        for head in range(half_heads):
            biases = jnp.where(row8 == head, bias_in[u * half_heads + head], biases)
        stage_bias[u] = biases
    net.await_peers()
    for copy in fetched[:3]:
        copy.wait()
    weight_net.start()
    token_net.start()
    bias_send = net.send(stage_bias, other_bias, net.lower())
    for u in range(2):
        stage_out[u, :, :HEAD_DIM] = jnp.zeros((block, HEAD_DIM), BF16)
        stage_out[u, :, HEAD_DIM:] = wo_t[:, u * half_cols : (u + 1) * half_cols]

    order_tables(places, spread, gather)
    every = places.every((1, places.all), 1)
    for late in range(2):
        at = places.own(late) + lax.broadcasted_iota(jnp.int32, (part, 1), 0)
        pos = places.position(at)
        start = doc_starts(pos, doc_ref)
        seen = (every <= pos) & (every >= start)
        allowed[late * part : (late + 1) * part, :] = jnp.where(seen, 0.0, MASKED).astype(BF16)

    weight_net.forward()
    token_net.forward()
    given_net.start()
    h_one[y] = norm(grad_attn[y].astype(F32), scale_one)
    token_net.finish()
    h_one[1 - y] = norm(grad_attn[1 - y].astype(F32), scale_one)
    weight_net.finish()

    for late in range(2):
        keyval[late, x, c] = dot_nn(h_one[late], w_attn[:, : 3 * LANES]).astype(BF16)
        kv_nets[late].start()
    bias_send.wait_recv()
    bias = jnp.where(weight_net.first, stage_bias[z % 2], other_bias[z % 2])[:, :1]
    for late in range(2):
        r = slice(late * part, (late + 1) * part)
        made = dot_nn(h_one[late], w_attn[:, 3 * LANES :])
        logit_parts[x, c, :, r] = made[:, LANES:].T[HEAD_DIM : HEAD_DIM + 8, :] + bias
        queries[r, :] = (made.astype(BF16).astype(F32) * HEAD_DIM ** (-0.5)).astype(BF16)
    logit_net.start()
    all_forget[net.group] = w_attn[:, 4 * LANES :].astype(F32).T[HEAD_DIM : HEAD_DIM + 8, :]
    forget_net.start(lambda index: all_forget.at[net.group], lambda index: all_forget.at[index])
    out_net.start()
    for copy in fetched[3:]:
        copy.wait()
    units_net.start()

    logit_net.forward()
    given_net.forward()
    logit_net.finish()
    for late in range(2):
        for xx in range(2):
            for cc in range(2):
                at = (late * 4 + xx * 2 + cc) * part
                logits[:, at : at + part] = logit_parts[xx, cc, :, late * part : (late + 1) * part]
    turned = logits[...]
    logs = jnp.minimum(turned, 0.0) - jnp.log(1.0 + jnp.exp(-jnp.abs(turned)))
    offsets[...] = running_sums(places, logs, spread, gather)
    kv_nets[0].forward()
    kv_nets[1].forward()
    out_net.forward()
    kv_nets[0].finish()

    lane = lax.broadcasted_iota(jnp.int32, (LANES, LANES), 1)
    first = (lane // HEAD_DIM) == 0
    for block in range(2 * part // LANES):
        r = slice(block * LANES, (block + 1) * LANES)
        late = (block * LANES) // part
        many = places.all // 2 * (late + 1)
        made, kept = [], []
        masses = jnp.zeros((LANES, LANES), F32)
        for head in range(3):
            tile_k, side_k = KEY_TILES[head]
            tile_v, side_v = VALUE_TILES[head]
            keys = keyval[: late + 1, :, :, :, tile_k * LANES : (tile_k + 1) * LANES]
            values = keyval[: late + 1, :, :, :, tile_v * LANES : (tile_v + 1) * LANES]
            keys, values = keys.reshape(many, LANES), values.reshape(many, LANES)
            scores = (
                dot_nt(only(tile_of(queries, r, tile_k), lane, side_k), keys)
                - offsets[head : head + 1, :many]
                + allowed[r, :many].astype(F32)
            )
            top = jnp.max(scores, axis=1, keepdims=True)
            probs = jnp.exp(scores - top)
            total = jnp.sum(probs, axis=1, keepdims=True)
            high = probs.astype(BF16)
            rest = (probs - high.astype(F32)).astype(BF16)
            share = 1.0 / total
            rounded = dot_nn(high, values)
            made.append(rounded * share)
            kept.append((rounded + dot_nn(rest, values)) * share)
            masses = jnp.where(lane == head, top + jnp.log(total), masses)
        mass[r, :] = masses
        mixed[r, :LANES] = jnp.where(first, 0.0, made[0]).astype(BF16)
        mixed[r, LANES:] = jnp.where(first, made[1], made[2]).astype(BF16)
        exact[r, :LANES] = jnp.where(first, 0.0, kept[0])
        exact[r, LANES:] = jnp.where(first, kept[1], kept[2])
        if block == 1:
            out_net.finish()
            kv_nets[1].finish()

    def project(late):
        rows = rows_of(late * part, part)
        for at in range(0, width, tile):
            cols = slice(at, at + tile)
            part_one[late, :, cols] = dot_nt(mixed[rows, :], w_out[cols, :]).astype(BF16)

    project(1 - y)
    for attn_sum in attn_sums:
        attn_sum.start()
    project(y)
    for attn_sum in attn_sums:
        attn_sum.middle()
    units_net.forward()
    earlier, net.pending = net.pending, []
    for k in range(2):
        total = own_tokens[pieces[k], :].astype(F32) + attn_sums[k].result()
        middle[pieces[k], :] = total
        normed_two[c, y, z, pieces[k], :] = norm(total, scale_two)
        two_nets[k].start()
    given_net.finish()
    two_nets[0].forward()
    units_net.finish()
    two_nets[0].finish()

    half_heads = half_cols
    tiles = [slice(at, at + tile) for at in range(0, width, tile)]

    query_net = CrossGather(net, lambda xx, cc: all_query.at[:, xx, cc])
    grad_net = CrossGather(net, lambda xx, cc: all_grad.at[:, xx, cc])
    stat_net = CrossGather(net, lambda xx, cc: stats.at[xx, cc])
    off_net = CrossGather(net, lambda xx, cc: off_parts.at[xx, cc])
    attn_nets = [RowGather(net, rows_at(grad_attn, k)) for k in range(2)]

    def own_parts(ref, k):
        return lambda yy, zz: ref.at[k, c, rows_of(yy * 4 * sub + zz * sub, sub), :]

    twos = [
        RowSum(net, own_parts(part_two, k), piece_of(two_up, k), piece_of(two_line, k))
        for k in range(2)
    ]
    outs = [
        RowSum(net, own_parts(part_out, k), piece_of(out_up, k), piece_of(out_line, k))
        for k in range(2)
    ]
    ones = [
        RowSum(net, rows_at(part_one, k), piece_of(one_up, k), piece_of(one_line, k))
        for k in range(2)
    ]
    ffn_net = HiddenSum(net, ffn_sum, ffn_side, ffn_final)
    late_net = WeightSum(net, late_sum, late_low, late_side, late_final)
    last_net = WeightSum(net, last_sum, last_low, last_side, last_final)
    early_net = WeightSum(net, early_sum, early_low, early_side, early_final)

    for late in range(2):
        all_query[late, x, c] = queries[late * part : (late + 1) * part, :]
    for wait in earlier:
        wait()
    query_net.start()

    def units_of(k):
        for cc in range(2):
            inputs = normed_two[cc, :, :, pieces[k], :].reshape(part, width)
            given = out_grads[cc, :, :, pieces[k], :].reshape(part, width)
            gate = dot_nn(inputs, w_ffn[:, :hidden])
            up = dot_nn(inputs, w_ffn[:, hidden : 2 * hidden])
            grad_act = dot_nn(given, w_ffn[:, 2 * hidden :])
            sigmoid = 1.0 / (1.0 + jnp.exp(-gate))
            silu = gate * sigmoid
            ffn_grads[k, cc, :, :hidden] = (
                grad_act * up * sigmoid * (1.0 + gate * (1.0 - sigmoid))
            ).astype(BF16)
            ffn_grads[k, cc, :, hidden : 2 * hidden] = (grad_act * silu).astype(BF16)
            ffn_grads[k, cc, :, 2 * hidden :] = (silu * up).astype(BF16)

    def lower_of(parts, recv, k, cols):
        def back(cc):
            for r in tiles:
                parts[k, cc, :, r] = dot_nt(ffn_grads[k, cc, :, cols], w_ffn[r, cols]).astype(BF16)

        back(1 - c)
        made = net.send(parts.at[k, 1 - c], recv.at[k], net.lower())
        back(c)
        return made

    def upper_of(made, parts, recv, k, sums):
        made.wait_recv()
        parts[k, c] = (parts[k, c].astype(F32) + recv[k].astype(F32)).astype(BF16)
        sums[k].start()

    def unit_grads(some):
        for cols in some:
            both = [0.0, 0.0]
            for k in range(2):
                left = normed_two[:, :, :, pieces[k], cols].reshape(2 * part, tile)
                right = ffn_grads[k].reshape(2 * part, 3 * hidden)
                both[0] = both[0] + dot_tn(left, right[:, : 2 * hidden])
                left = out_grads[:, :, :, pieces[k], cols].reshape(2 * part, tile)
                both[1] = both[1] + dot_tn(left, right[:, 2 * hidden :])
            ffn_sum[cols, : 2 * hidden] = both[0].astype(BF16)
            ffn_sum[cols, 2 * hidden :] = both[1].astype(BF16)

    units_of(0)
    two_nets[1].forward()
    to_lower = slice(0, 2 * hidden)
    first_low = lower_of(part_two, two_low, 0, to_lower)
    two_nets[1].finish()
    units_of(1)
    upper_of(first_low, part_two, two_low, 0, twos)
    second_low = lower_of(part_two, two_low, 1, to_lower)
    twos[0].middle()
    upper_of(second_low, part_two, two_low, 1, twos)
    unit_grads(tiles[:3])
    twos[1].middle()
    unit_grads(tiles[3:])
    query_net.forward()
    ffn_net.start()
    grad_middle = []
    gain_two_part = 0.0
    for k in range(2):
        back_two, part_gain = norm_grad(twos[k].result(), middle[pieces[k], :], scale_two)
        gain_two_part = gain_two_part + part_gain
        grad_middle.append(out_grads[c, y, z, pieces[k], :].astype(F32) + back_two)
        grad_attn[y, rows_of(z * chunk + k * sub, sub), :] = grad_middle[k].astype(BF16)
        attn_nets[k].start()
    to_out = slice(2 * hidden, 3 * hidden)
    out_sends = [lower_of(part_out, out_low, 0, to_out), None]
    attn_nets[0].forward()
    out_sends[1] = lower_of(part_out, out_low, 1, to_out)
    every = places.every((1, places.all), 1)
    own_pos = [
        places.position(places.own(late) + lax.broadcasted_iota(jnp.int32, (part, 1), 0))
        for late in range(2)
    ]
    attn_nets[1].forward()
    attn_nets[0].finish()
    query_net.finish()
    attn_nets[1].finish()

    lane = lax.broadcasted_iota(jnp.int32, (part, LANES), 1)
    for late in range(2):
        r = slice(late * part, (late + 1) * part)
        made = dot_nn(grad_attn[late], w_out[...])
        grad_heads[r, :] = made.astype(BF16)
        all_grad[late, x, c] = grad_heads[r, :]
    grad_net.start()
    for late in range(2):
        r = slice(late * part, (late + 1) * part)
        delta = jnp.zeros((part, LANES), F32)
        for head, (tile_o, side_o) in enumerate(OUT_TILES):
            product = tile_of(grad_heads, r, tile_o).astype(F32) * tile_of(exact, r, tile_o)
            inner = jnp.sum(only(product, lane, side_o), axis=1, keepdims=True)
            delta = jnp.where(lane == head, inner, delta)
        grad_offs[r, :] = delta
    stats[x, c, :8, :] = mass[...].T[:8, :]
    stats[x, c, 8:, :] = grad_offs[...].T[:8, :]
    stat_net.start()

    for cols in tiles:
        left = grad_attn[:, :, cols].reshape(2 * part, tile)
        early_sum[cols, :] = dot_tn(left, mixed[...]).astype(BF16)
    early_net.start()
    for k in range(2):
        upper_of(out_sends[k], part_out, out_low, k, outs)
    ffn_net.second()

    lane = lax.broadcasted_iota(jnp.int32, (LANES, LANES), 1)
    first = (lane // HEAD_DIM) == 0
    for block in range(2 * part // LANES):
        r = slice(block * LANES, (block + 1) * LANES)
        late = (block * LANES) // part
        many = places.all // 2 * (late + 1)
        made = []
        sums = jnp.zeros((LANES, LANES), F32)
        for head in range(3):
            tile_k, side_k = KEY_TILES[head]
            tile_v, side_v = VALUE_TILES[head]
            tile_o, side_o = OUT_TILES[head]
            keys = keyval[: late + 1, :, :, :, tile_k * LANES : (tile_k + 1) * LANES]
            values = keyval[: late + 1, :, :, :, tile_v * LANES : (tile_v + 1) * LANES]
            keys, values = keys.reshape(many, LANES), values.reshape(many, LANES)
            scores = (
                dot_nt(only(tile_of(queries, r, tile_k), lane, side_k), keys)
                - offsets[head : head + 1, :many]
                + allowed[r, :many].astype(F32)
            )
            probs = jnp.exp(scores - mass[r, head : head + 1])
            grad_probs = dot_nt(only(tile_of(grad_heads, r, tile_o), lane, side_o), values)
            grad_scores = (probs * (grad_probs - grad_offs[r, head : head + 1])).astype(BF16)
            made.append(dot_nn(grad_scores, keys) * HEAD_DIM ** (-0.5))
            row_sum = jnp.sum(grad_scores.astype(F32), axis=1, keepdims=True)
            sums = jnp.where(lane == head, row_sum, sums)
        grad_qkv[r, 3 * LANES : 4 * LANES] = jnp.where(first, made[0], made[1]).astype(BF16)
        grad_qkv[r, 4 * LANES :] = jnp.where(first, made[2], 0.0).astype(BF16)
        grad_offs[r, :] = sums
        if block == 0:
            grad_net.forward()
            stat_net.forward()
        if block == 1:
            for out in outs:
                out.middle()
            early_net.second()

    starts = doc_starts(every, doc_ref)
    for late in range(2):
        seen = (own_pos[late] <= every) & (own_pos[late] >= starts)
        allowed[late * part : (late + 1) * part, :] = jnp.where(seen, 0.0, MASKED).astype(BF16)
    stat_net.finish()
    grad_net.finish()
    for late in range(2):
        for xx in range(2):
            for cc in range(2):
                at = (late * 4 + xx * 2 + cc) * part
                piece = slice(late * part, (late + 1) * part)
                every_off[0, :, at : at + part] = stats[xx, cc, :8, piece]
                every_off[1, :, at : at + part] = stats[xx, cc, 8:, piece]

    own_offs = [
        to_columns(offsets[:, pl.ds(pl.multiple_of(places.own(late), LANES), part)])
        for late in range(2)
    ]
    for block in range(2 * part // LANES):
        r = slice(block * LANES, (block + 1) * LANES)
        late = (block * LANES) // part
        within = slice(block * LANES - late * part, (block + 1) * LANES - late * part)
        many = places.all // 2 * (2 - late)
        lanes = slice(places.all - many, places.all)
        keys_made, values_made = [], []
        sums = jnp.zeros((LANES, LANES), F32)
        for head in range(3):
            tile_k, side_k = KEY_TILES[head]
            tile_v, side_v = VALUE_TILES[head]
            tile_o, side_o = OUT_TILES[head]
            asked = all_query[late:, :, :, :, tile_k * LANES : (tile_k + 1) * LANES]
            given = all_grad[late:, :, :, :, tile_o * LANES : (tile_o + 1) * LANES]
            asked, given = asked.reshape(many, LANES), given.reshape(many, LANES)
            key = keyval[late, x, c, within, tile_k * LANES : (tile_k + 1) * LANES]
            value = keyval[late, x, c, within, tile_v * LANES : (tile_v + 1) * LANES]
            scores = (
                dot_nt(only(key, lane, side_k), asked)
                - own_offs[late][within, head : head + 1]
                + allowed[r, lanes].astype(F32)
            )
            probs = jnp.exp(scores - every_off[0, head : head + 1, lanes])
            grad_probs = dot_nt(only(value, lane, side_v), given)
            grad_scores = (probs * (grad_probs - every_off[1, head : head + 1, lanes])).astype(
                BF16
            )
            keys_made.append(dot_nn(grad_scores, asked))
            values_made.append(dot_nn(probs.astype(BF16), given))
            col_sum = jnp.sum(grad_scores.astype(F32), axis=1, keepdims=True)
            sums = jnp.where(lane == head, col_sum, sums)
        for at, (left, right) in enumerate(
            (
                (keys_made[0], keys_made[1]),
                (keys_made[2], values_made[0]),
                (values_made[1], values_made[2]),
            )
        ):
            grad_qkv[r, at * LANES : (at + 1) * LANES] = jnp.where(first, left, right).astype(BF16)
        grad_offs[r, :] = grad_offs[r, :] - sums
        if block == 1:
            early_net.third()
    off_parts[x, c] = grad_offs[...].T[:8, :]
    off_net.start()

    def back(late):
        rows = rows_of(late * part, part)
        for r in tiles:
            part_one[late, :, r] = dot_nt(grad_qkv[rows, :], w_attn[r, :]).astype(BF16)

    back(1 - y)
    for one in ones:
        one.start()
    back(y)
    off_net.forward()
    cut = late_sum.shape[1]
    for cols in tiles:
        left = h_one[:, :, cols].reshape(2 * part, tile)
        late_sum[cols, :] = dot_tn(left, grad_qkv[:, :cut]).astype(BF16)
    late_net.start()
    ones[0].middle()
    off_net.finish()
    for late in range(2):
        for xx in range(2):
            for cc in range(2):
                at = (late * 4 + xx * 2 + cc) * part
                every_off[0, :, at : at + part] = off_parts[
                    xx, cc, :, late * part : (late + 1) * part
                ]
    given = every_off[0]
    whole = jnp.sum(given, axis=1, keepdims=True)
    grad_logs = whole - running_sums(places, given, spread, gather) + given
    grad_logits = grad_logs / (1.0 + jnp.exp(logits[...]))
    every_off[1] = grad_logits

    def rows_for(index):
        at = places.own(index % 2) + (index // 4) * LANES
        return every_off.at[1, :, pl.ds(pl.multiple_of(at, LANES), LANES)]

    logit_back.start(rows_for, lambda index: own_logits.at[index])
    own_logits[net.group] = rows_for(net.group)[...]
    ones[1].middle()
    late_net.second()
    for late in range(2):
        r = slice(late * part, (late + 1) * part)
        mine = every_off[1, :, pl.ds(pl.multiple_of(places.own(late), LANES), part)]
        held = grad_qkv[r, cut:]
        lane = lax.broadcasted_iota(jnp.int32, (part, LANES), 1)
        grad_qkv[r, cut:] = jnp.where(
            lane // HEAD_DIM == 0, held, to_columns(mine, HEAD_DIM).astype(BF16)
        )
    for cols in tiles:
        left = h_one[:, :, cols].reshape(2 * part, tile)
        last_sum[cols, :] = dot_tn(left, grad_qkv[:, cut:]).astype(BF16)
    last_net.start()
    late_net.third()
    logit_back.finish(lambda index: own_logits.at[index])
    forget_net.finish(lambda index: all_forget.at[index])
    held = own_logits[...].reshape(8 * 8, LANES)
    held = jnp.where(z % 2 == 0, held[:, :chunk], held[:, chunk:]).astype(BF16)
    forget_part = dot_tn(held, all_forget[...].reshape(8 * 8, width).astype(BF16))
    last_net.second()
    for k in range(2):
        layer_out[rows_of((2 * y + c) * chunk + k * sub, sub), :] = (
            middle[pieces[k], :] + outs[k].result()
        ).astype(BF16)
    layer_second = gather_quarters(net, layer_out)
    gain_one_part = 0.0
    for k in range(2):
        back_one, part_gain = norm_grad(
            ones[k].result() + forget_part[pieces[k], :],
            own_tokens[pieces[k], :].astype(F32),
            scale_one,
        )
        gain_one_part = gain_one_part + part_gain
        tokens_grad[rows_of((2 * y + c) * chunk + k * sub, sub), :] = (
            grad_middle[k] + back_one
        ).astype(BF16)
    grad_second = gather_quarters(net, tokens_grad)
    cells = width // 4
    gain_mine = gain_parts.at[z * 2 + x]
    gain_mine[:, :cells] = jnp.concatenate(
        [g[:, k * cells : (k + 1) * cells] for g in (gain_one_part, gain_two_part) for k in range(4)],
        axis=0,
    )
    gain_mine[:, cells:] = jnp.broadcast_to(
        jnp.sum(grad_logits, axis=1, keepdims=True), (8, LANES)
    )
    gain_net.start(lambda index: gain_mine, lambda index: gain_parts.at[index])
    last_net.third()
    layer_last = layer_second()
    grad_last = grad_second()

    gain_net.finish(lambda index: gain_parts.at[index])
    total = gain_parts[0, :, :cells]
    for index in range(1, 8):
        total = total + gain_parts[index, :, :cells]
    gain_swap[y * 2 + c] = total
    last_gain.start(lambda index: gain_swap.at[y * 2 + c], lambda index: gain_swap.at[index])
    for u in range(2):
        bias_grad[u] = gain_parts[(2 * c + u) * 2 + x, :, cells:]

    ffn_net.finish()
    early_net.finish()
    last_gain.finish(lambda index: gain_swap.at[index])
    total = gain_swap[0]
    for index in range(1, 4):
        total = total + gain_swap[index]
    gains[...] = total

    late_net.finish()
    last_net.finish()
    layer_last()
    grad_last()
    for part_net in (weight_net, out_net, late_net, last_net, early_net, net):
        part_net.drain()


def narrow_kernel(
    layer,
    tokens,
    gains,
    biases,
    late,
    last,
    early,
    units,
    layer_out,
    tokens_grad,
    gain_one,
    g_query,
    g_key,
    g_value,
    g_forget,
    g_bias,
    g_out,
    gain_two,
    g_gate,
    g_up,
    g_down,
):
    layer_out[...] = layer[...]
    tokens_grad[...] = tokens[...]
    for k, ref in enumerate((gain_one, gain_two)):
        ref[...] = jnp.concatenate(
            [gains[4 * k + at : 4 * k + at + 1, :] for at in range(4)], axis=1
        )[0]
    half = g_query.shape[1] // 2
    heads = half // HEAD_DIM
    hidden = units.shape[2] // 3
    block = g_query.shape[0]
    for u in range(2):
        cols = slice(u * half, (u + 1) * half)
        got = late[u].astype(F32)
        rest = last[u].astype(F32)
        g_key[:, cols] = got[:, :half]
        g_value[:, cols] = got[:, half : 2 * half]
        g_query[:, cols] = jnp.concatenate([got[:, 2 * half :], rest[:, :HEAD_DIM]], axis=1)
        g_out[:, cols] = early[u, :, HEAD_DIM:].astype(F32)
        padded = jnp.concatenate([rest, jnp.zeros((2 * LANES - block, LANES), F32)], axis=0)
        g_forget[u * heads : (u + 1) * heads, :] = padded.T[HEAD_DIM : HEAD_DIM + heads, :block]
    each = jnp.concatenate([biases[0, :heads, :], biases[1, :heads, :]], axis=0)
    g_bias[...] = each
    for zz in range(4):
        cols = slice(zz * hidden, (zz + 1) * hidden)
        for index, ref in enumerate((g_gate, g_up, g_down)):
            ref[:, cols] = units[zz, :, index * hidden : (index + 1) * hidden].astype(F32)


VMEM = pl.BlockSpec(memory_space=pltpu.VMEM)
SMEM = pl.BlockSpec(memory_space=pltpu.SMEM)
HBM = pl.BlockSpec(memory_space=pl.ANY)


def shapes_of(made):
    return [jax.ShapeDtypeStruct(*m) for m in made]


def layer_shapes(rows, width, heads, hidden):
    chunk = rows // 4
    part = 4 * chunk
    every = 32 * chunk
    block = width // 8
    attn = (3 * heads * HEAD_DIM // 2) + HEAD_DIM
    cut = attn - LANES
    outs = [
        ((rows, width), BF16),
        ((rows, width), BF16),
        ((8, width // 4), F32),
        ((2, 8, LANES), F32),
        ((2, block, cut), BF16),
        ((2, block, LANES), BF16),
        ((2, block, 2 * LANES), BF16),
        ((4, block, 3 * hidden), BF16),
    ]

    def weight_sum(columns):
        return [
            ((width, columns), BF16),
            ((width // 2, columns), BF16),
            ((2, block, columns), BF16),
        ]

    row_sum = [((2, part, width), BF16), ((4, chunk, width), BF16), ((4, chunk, width), BF16)]
    scratch = [
        ((2, block, attn), BF16),
        ((2, block, 2 * LANES), BF16),
        ((2, 8, LANES), F32),
        ((2, 8, LANES), F32),
        ((2, part, width), BF16),
        ((2 * part, every), BF16),
        ((every, LANES), F32),
        ((every // chunk, every), F32),
        ((2, 2, 8, 2 * part), F32),
        ((2 * part, 2 * LANES), BF16),
        ((2, 2, 2, part, 3 * LANES), BF16),
        ((8, every), F32),
        ((2 * part, LANES), F32),
        ((8, every), F32),
        ((2 * part, 2 * LANES), BF16),
        ((2 * part, 2 * LANES), F32),
        ((chunk, width), F32),
        ((2, 2, 4, chunk, width), BF16),
        ((2, 2, 4, chunk, width), BF16),
        ((width, attn), BF16),
        ((width, 2 * LANES), BF16),
        ((width, 3 * hidden), BF16),
        ((2, 2, 2, part, 2 * LANES), BF16),
        ((2, 2, 2, part, 2 * LANES), BF16),
        ((2, 2, part, 3 * hidden), BF16),
        ((2, 2, part, width), BF16),
        ((2, 2, part, width), BF16),
        *row_sum,
        *row_sum,
        ((width, 3 * hidden), BF16),
        ((4, block, 3 * hidden), BF16),
        *weight_sum(cut),
        *weight_sum(LANES),
        *weight_sum(2 * LANES),
        ((2, part, width), BF16),
        ((2 * part, 2 * LANES), BF16),
        ((2, 2, 16, 2 * part), F32),
        ((2, 2, 8, 2 * part), F32),
        ((2, 8, every), F32),
        ((2 * part, attn), BF16),
        ((2 * part, LANES), F32),
        *row_sum,
        ((8, 8, width // 4 + LANES), F32),
        ((4, 8, width // 4), F32),
        ((chunk, width), BF16),
        ((8, 8, width), F32),
        ((8, 8, LANES), F32),
    ]
    return outs, scratch


def kernel_body(
    tokens,
    attn_gain,
    query_weight,
    key_weight,
    value_weight,
    forget_weight,
    forget_bias,
    out_weight,
    ffn_gain,
    gate_weight,
    up_weight,
    down_weight,
    doc_lengths,
    out_grad,
):
    heads = forget_bias.shape[0]
    rows, width = tokens.shape
    block, units = gate_weight.shape
    cols = query_weight.shape[1]
    outs, scratch = layer_shapes(rows, width, heads, units // 4)
    made = pl.pallas_call(
        layer_kernel,
        out_shape=shapes_of(outs),
        in_specs=[HBM] * 2 + [VMEM] * 6 + [SMEM] + [VMEM] + [HBM] * 3 + [SMEM],
        out_specs=[VMEM] * len(outs),
        scratch_shapes=[pltpu.VMEM(*m) for m in scratch] + [pltpu.SemaphoreType.DMA((15,)), pltpu.SemaphoreType.DMA((640,))],
        compiler_params=pltpu.CompilerParams(
            collective_id=0, has_side_effects=True, vmem_limit_bytes=63 << 20
        ),
    )(
        tokens,
        out_grad,
        attn_gain,
        ffn_gain,
        query_weight,
        key_weight,
        value_weight,
        forget_weight.T,
        forget_bias,
        out_weight.T,
        gate_weight,
        up_weight,
        down_weight.T,
        doc_lengths,
    )
    finals = [
        ((rows, width), BF16),
        ((rows, width), BF16),
        ((width,), F32),
        ((block, cols), F32),
        ((block, cols), F32),
        ((block, cols), F32),
        ((heads, block), F32),
        ((heads, LANES), F32),
        ((block, cols), F32),
        ((width,), F32),
        ((block, units), F32),
        ((block, units), F32),
        ((block, units), F32),
    ]
    final = pl.pallas_call(
        narrow_kernel,
        out_shape=shapes_of(finals),
        in_specs=[VMEM] * len(outs),
        out_specs=[VMEM] * len(finals),
        compiler_params=pltpu.CompilerParams(vmem_limit_bytes=63 << 20),
    )(*made)
    return (
        *final[:6],
        final[6].T,
        final[7][:, 0],
        final[8].T,
        *final[9:12],
        final[12].T,
    )


def kernels_fit(tokens, forget_bias, gate_weight):
    rows, width = tokens.shape
    heads = forget_bias.shape[0]
    return (
        lax.axis_size("seq") == 8
        and lax.axis_size("head") == 4
        and heads == 6
        and rows == 2 * LANES
        and width % 256 == 0
        and gate_weight.shape[1] % (4 * LANES) == 0
        and width * gate_weight.shape[1] <= (1536 * 1024)
    )


def unchanged(carried):
    return carried


def contract_rows(left, right):
    return lax.dot_general(
        left, right, (((0,), (0,)), ((), ())), preferred_element_type=jnp.float32
    )


def contract_cols(left, right):
    return lax.dot_general(
        left, right, (((1,), (1,)), ((), ())), preferred_element_type=jnp.float32
    )


def norm_rows(values_in, gain):
    inverse = lax.rsqrt(jnp.mean(values_in * values_in, axis=-1, keepdims=True) + EPSILON)
    normed = values_in * inverse
    return (normed, inverse, normed * gain)


def norm_back(grad_in, normed, inverse, gain):
    scaled = grad_in * gain
    inner = jnp.mean(scaled * normed, axis=-1, keepdims=True)
    return (inverse * (scaled - normed * inner), jnp.sum(grad_in * normed, axis=0))


def doc_index(positions, doc_ends):
    return jnp.sum((positions[:, None] >= doc_ends[None, :]).astype(jnp.int32), axis=1)


def stored_positions(rows, n_seq, local_rows):
    half_rows = local_rows // 2
    device_of = rows // local_rows
    within = rows % local_rows
    group_of = jnp.where(within < half_rows, device_of, 2 * n_seq - 1 - device_of)
    return group_of * half_rows + within % half_rows


def block_scores(
    query_heads, key_heads, query_offsets, key_offsets, query_pos, key_pos, query_docs, key_docs
):
    raw_scores = jnp.einsum(
        "qhd,khd->hqk", query_heads, key_heads, preferred_element_type=jnp.float32
    )
    scores = (
        raw_scores * HEAD_DIM ** (-0.5) + query_offsets.T[:, :, None] - key_offsets.T[:, None, :]
    )
    allowed = (query_docs[:, None] == key_docs[None, :]) & (key_pos[None, :] <= query_pos[:, None])
    return (jnp.where(allowed[None], scores, MASKED), allowed)


def piece_grads(
    query_heads,
    grad_heads,
    log_mass,
    row_delta,
    query_offsets,
    key_heads,
    value_heads,
    key_offsets,
    query_pos,
    key_pos,
    query_docs,
    key_docs,
):
    scores, allowed = block_scores(
        query_heads, key_heads, query_offsets, key_offsets, query_pos, key_pos, query_docs, key_docs
    )
    probs = jnp.where(allowed[None], jnp.exp(scores - log_mass[:, :, None]), 0.0)
    grad_probs = jnp.einsum(
        "qhd,khd->hqk", grad_heads, value_heads, preferred_element_type=jnp.float32
    )
    grad_scores = (probs * (grad_probs - row_delta[:, :, None])).astype(jnp.bfloat16)
    score_sums = grad_scores.astype(jnp.float32)
    query_rows = query_heads.shape[0]
    key_rows = key_heads.shape[0]
    grad_query = jnp.einsum(
        "hqk,khd->qhd", grad_scores, key_heads, preferred_element_type=jnp.float32
    ).reshape(query_rows, -1)
    grad_key = (
        jnp.einsum("hqk,qhd->khd", grad_scores, query_heads, preferred_element_type=jnp.float32)
        * HEAD_DIM ** (-0.5)
    ).reshape(key_rows, -1)
    grad_value = jnp.einsum(
        "hqk,qhd->khd", probs.astype(jnp.bfloat16), grad_heads, preferred_element_type=jnp.float32
    ).reshape(key_rows, -1)
    return (
        grad_query,
        jnp.sum(score_sums, axis=2).T,
        grad_key,
        grad_value,
        -jnp.sum(score_sums, axis=1).T,
    )


def plain_body(
    tokens,
    attn_gain,
    query_weight,
    key_weight,
    value_weight,
    forget_weight,
    forget_bias,
    out_weight,
    ffn_gain,
    gate_weight,
    up_weight,
    down_weight,
    doc_lengths,
    out_grad,
):
    local_rows = tokens.shape[0]
    local_heads = forget_bias.shape[0]
    head_cols = local_heads * HEAD_DIM
    n_seq = lax.axis_size("seq")
    my_index = lax.axis_index("seq")
    first_row = my_index * local_rows
    docs = doc_lengths.shape[0]
    doc_ends = jnp.sum(jnp.where(jnp.tri(docs, dtype=jnp.bool_), doc_lengths[None, :], 0), axis=1)
    local_pos = stored_positions(
        first_row + jnp.arange(local_rows, dtype=jnp.int32), n_seq, local_rows
    )
    local_docs = doc_index(local_pos, doc_ends)
    pos_low = jnp.min(local_pos)
    pos_high = jnp.max(local_pos)
    doc_low = jnp.min(local_docs)
    doc_high = jnp.max(local_docs)
    hidden = gate_weight.shape[1]
    forget_pad = jnp.pad(forget_weight, ((0, 0), (0, 128 - local_heads)))
    w_attn = lax.all_gather(
        jnp.concatenate([query_weight, key_weight, value_weight, forget_pad], axis=1),
        "seq",
        axis=0,
        tiled=True,
    )
    w_rest = lax.all_gather(
        jnp.concatenate([out_weight.T, gate_weight, up_weight, down_weight.T], axis=1),
        "seq",
        axis=0,
        tiled=True,
    )
    w_query = w_attn[:, :head_cols]
    w_key = w_attn[:, head_cols : 2 * head_cols]
    w_value = w_attn[:, 2 * head_cols : 3 * head_cols]
    w_forget = w_attn[:, 3 * head_cols : 3 * head_cols + local_heads]
    w_out_t = w_rest[:, :head_cols]
    w_gate = w_rest[:, head_cols : head_cols + hidden]
    w_up = w_rest[:, head_cols + hidden : head_cols + 2 * hidden]
    w_down_t = w_rest[:, head_cols + 2 * hidden :]
    inputs = tokens.astype(jnp.float32)
    normed_one, inverse_one, scaled_one = norm_rows(inputs, attn_gain)
    h_one = scaled_one.astype(jnp.bfloat16)
    query_flat = jnp.dot(h_one, w_query, preferred_element_type=jnp.float32).astype(jnp.bfloat16)
    key_flat = jnp.dot(h_one, w_key, preferred_element_type=jnp.float32).astype(jnp.bfloat16)
    value_flat = jnp.dot(h_one, w_value, preferred_element_type=jnp.float32).astype(jnp.bfloat16)
    forget_logit = jnp.dot(h_one, w_forget, preferred_element_type=jnp.float32) + forget_bias
    log_forget_all = lax.all_gather(jax.nn.log_sigmoid(forget_logit), "seq", axis=0, tiled=True)
    all_pos = stored_positions(
        jnp.arange(n_seq * local_rows, dtype=jnp.int32), n_seq, local_rows
    )
    earlier = (all_pos[None, :] <= all_pos[:, None]).astype(jnp.float32)
    offsets_all = jnp.dot(earlier, log_forget_all, precision=HIGHEST)
    offsets = lax.dynamic_slice_in_dim(offsets_all, first_row, local_rows, 0)
    query_heads = query_flat.reshape(local_rows, local_heads, HEAD_DIM)
    key_heads = key_flat.reshape(local_rows, local_heads, HEAD_DIM)
    value_heads = value_flat.reshape(local_rows, local_heads, HEAD_DIM)

    def key_range(piece_rows):
        key_pos = stored_positions(jnp.arange(piece_rows, dtype=jnp.int32), n_seq, local_rows)
        key_docs = doc_index(key_pos, doc_ends)
        is_live = (
            (jnp.min(key_pos) <= pos_high)
            & (jnp.max(key_docs) >= doc_low)
            & (jnp.min(key_docs) <= doc_high)
        )
        return (key_pos, key_docs, offsets_all, is_live)

    mass_state = (
        jnp.full((local_heads, local_rows), MASKED, jnp.float32),
        jnp.zeros((local_heads, local_rows), jnp.float32),
    )
    gathered = lax.all_gather(
        jnp.concatenate([key_flat, value_flat, query_flat], axis=1), "seq", axis=0, tiled=True
    )
    key_block = gathered[:, :head_cols]
    piece_rows = key_block.shape[0]
    key_pos, key_docs, key_offsets, is_live = key_range(piece_rows)

    def mass_update(carried_in):
        running_max, running_sum = carried_in
        scores, allowed = block_scores(
            query_heads,
            key_block.reshape(piece_rows, local_heads, HEAD_DIM),
            offsets,
            key_offsets,
            local_pos,
            key_pos,
            local_docs,
            key_docs,
        )
        new_max = jnp.maximum(running_max, jnp.max(scores, axis=2))
        weights = jnp.where(allowed[None], jnp.exp(scores - new_max[:, :, None]), 0.0)
        return (new_max, jnp.sum(weights, axis=2))

    running_max, running_sum = lax.cond(is_live, mass_update, unchanged, mass_state)
    log_mass = running_max + jnp.log(running_sum)
    start_state = (
        jnp.zeros((local_heads, local_rows, HEAD_DIM), jnp.float32),
        jnp.zeros((local_heads, local_rows, HEAD_DIM), jnp.float32),
    )
    attend_key_block = key_block
    value_block = gathered[:, head_cols : 2 * head_cols]
    attend_piece_rows = attend_key_block.shape[0]
    attend_key_pos, attend_key_docs, attend_key_offsets, is_live = key_range(attend_piece_rows)

    def attend_update(carried_in):
        scores, allowed = block_scores(
            query_heads,
            attend_key_block.reshape(attend_piece_rows, local_heads, HEAD_DIM),
            offsets,
            attend_key_offsets,
            local_pos,
            attend_key_pos,
            local_docs,
            attend_key_docs,
        )
        probs = jnp.where(allowed[None], jnp.exp(scores - log_mass[:, :, None]), 0.0)
        probs_low = probs.astype(jnp.bfloat16)
        remainder = (probs - probs_low.astype(jnp.float32)).astype(jnp.bfloat16)
        value_piece = value_block.reshape(attend_piece_rows, local_heads, HEAD_DIM)
        rounded_acc = jnp.einsum(
            "hqk,khd->hqd", probs_low, value_piece, preferred_element_type=jnp.float32
        )
        remainder_acc = jnp.einsum(
            "hqk,khd->hqd", remainder, value_piece, preferred_element_type=jnp.float32
        )
        return (rounded_acc, remainder_acc)

    rounded_acc, remainder_acc = lax.cond(is_live, attend_update, unchanged, start_state)
    attended_rows = rounded_acc.transpose(1, 0, 2)
    exact_rows = (rounded_acc + remainder_acc).transpose(1, 0, 2)
    mixed = attended_rows.reshape(local_rows, head_cols).astype(jnp.bfloat16)
    attn_part = contract_cols(mixed, w_out_t)
    middle = inputs + lax.psum(attn_part, "head")
    normed_two, inverse_two, scaled_two = norm_rows(middle, ffn_gain)
    h_two = scaled_two.astype(jnp.bfloat16)
    gate_value = jnp.dot(h_two, w_gate, preferred_element_type=jnp.float32)
    up_value = jnp.dot(h_two, w_up, preferred_element_type=jnp.float32)
    gate_sigmoid = jax.nn.sigmoid(gate_value)
    gate_silu = gate_value * gate_sigmoid
    activation = (gate_silu * up_value).astype(jnp.bfloat16)
    ffn_part = contract_cols(activation, w_down_t)
    layer_out = (
        middle + lax.psum(ffn_part.astype(jnp.bfloat16), "head").astype(jnp.float32)
    ).astype(jnp.bfloat16)
    grad_act = jnp.dot(out_grad, w_down_t, preferred_element_type=jnp.float32)
    grad_gate = (
        grad_act * up_value * gate_sigmoid * (1.0 + gate_value * (1.0 - gate_sigmoid))
    ).astype(jnp.bfloat16)
    grad_up = (grad_act * gate_silu).astype(jnp.bfloat16)
    part_two = contract_cols(grad_gate, w_gate) + contract_cols(grad_up, w_up)
    grad_two = lax.psum(part_two, "head")
    back_two, gain_two = norm_back(grad_two, normed_two, inverse_two, ffn_gain)
    grad_middle = out_grad.astype(jnp.float32) + back_two
    grad_attn = grad_middle.astype(jnp.bfloat16)
    grad_mixed = jnp.dot(grad_attn, w_out_t, preferred_element_type=jnp.float32).astype(
        jnp.bfloat16
    )
    grad_heads = grad_mixed.reshape(local_rows, local_heads, HEAD_DIM)
    row_delta = jnp.sum(grad_heads.astype(jnp.float32) * exact_rows, axis=2).T
    back_state = (
        jnp.zeros((local_rows, head_cols), jnp.float32),
        jnp.zeros((local_rows, local_heads), jnp.float32),
    )
    back_key_block = key_block
    back_value_block = value_block
    back_piece_rows = back_key_block.shape[0]
    back_key_pos, back_key_docs, back_key_offsets, is_live = key_range(back_piece_rows)

    def back_update(carried_in):
        terms = piece_grads(
            query_heads,
            grad_heads,
            log_mass,
            row_delta,
            offsets,
            back_key_block.reshape(back_piece_rows, local_heads, HEAD_DIM),
            back_value_block.reshape(back_piece_rows, local_heads, HEAD_DIM),
            back_key_offsets,
            local_pos,
            back_key_pos,
            local_docs,
            back_key_docs,
        )
        return (terms[0], terms[1])

    grad_query, grad_query_off = lax.cond(is_live, back_update, unchanged, back_state)
    stats = lax.all_gather(
        jnp.concatenate([log_mass.T, row_delta.T], axis=1), "seq", axis=0, tiled=True
    )
    stats_mass, stats_delta = stats[:, :local_heads], stats[:, local_heads:]
    key_state = (
        jnp.zeros((local_rows, head_cols), jnp.float32),
        jnp.zeros((local_rows, head_cols), jnp.float32),
        jnp.zeros((local_rows, local_heads), jnp.float32),
    )
    piece_query = gathered[:, 2 * head_cols :]
    piece_grad = lax.all_gather(grad_mixed, "seq", axis=0, tiled=True)
    key_piece_rows = piece_query.shape[0]
    piece_pos = stored_positions(jnp.arange(key_piece_rows, dtype=jnp.int32), n_seq, local_rows)
    piece_docs = doc_index(piece_pos, doc_ends)
    is_live = (
        (pos_low <= jnp.max(piece_pos))
        & (jnp.max(piece_docs) >= doc_low)
        & (jnp.min(piece_docs) <= doc_high)
    )

    def key_update(carried_in):
        piece_mass = stats_mass.T
        piece_delta = stats_delta.T
        terms = piece_grads(
            piece_query.reshape(key_piece_rows, local_heads, HEAD_DIM),
            piece_grad.reshape(key_piece_rows, local_heads, HEAD_DIM),
            piece_mass,
            piece_delta,
            offsets_all,
            key_heads,
            value_heads,
            offsets,
            piece_pos,
            local_pos,
            piece_docs,
            local_docs,
        )
        return (terms[2], terms[3], terms[4])

    grad_key, grad_value, grad_key_off = lax.cond(is_live, key_update, unchanged, key_state)
    grad_query_low = (grad_query * HEAD_DIM ** (-0.5)).astype(jnp.bfloat16)
    grad_key_low = grad_key.astype(jnp.bfloat16)
    grad_value_low = grad_value.astype(jnp.bfloat16)
    grad_offsets = grad_query_off + grad_key_off
    grad_off_all = lax.all_gather(grad_offsets, "seq", axis=0, tiled=True)
    later = (all_pos[None, :] >= local_pos[:, None]).astype(jnp.float32)
    grad_log = jnp.dot(later, grad_off_all, precision=HIGHEST)
    grad_logit = grad_log * jax.nn.sigmoid(-forget_logit)
    forget_table = w_forget.astype(jnp.float32)
    part_one = (
        contract_cols(grad_query_low, w_query)
        + contract_cols(grad_key_low, w_key)
        + contract_cols(grad_value_low, w_value)
        + lax.dot_general(grad_logit, forget_table, (((1,), (1,)), ((), ())), precision=HIGHEST)
    )
    grad_one = lax.psum(part_one.astype(jnp.bfloat16), "head").astype(jnp.float32)
    back_one, gain_one = norm_back(grad_one, normed_one, inverse_one, attn_gain)
    tokens_grad = (grad_middle + back_one).astype(jnp.bfloat16)
    forget_term = lax.dot_general(
        h_one.astype(jnp.float32), grad_logit, (((0,), (0,)), ((), ())), precision=HIGHEST
    )
    scatter_cols = [
        contract_rows(grad_attn, mixed),
        contract_rows(h_two, grad_gate),
        contract_rows(h_two, grad_up),
        contract_rows(out_grad, activation),
        contract_rows(h_one, grad_query_low),
        contract_rows(h_one, grad_key_low),
        contract_rows(h_one, grad_value_low),
        jnp.pad(forget_term, ((0, 0), (0, 128 - local_heads))),
    ]
    first_sum = lax.psum_scatter(
        jnp.concatenate([t.astype(jnp.bfloat16) for t in scatter_cols[:4]], axis=1),
        "seq",
        scatter_dimension=0,
        tiled=True,
    ).astype(jnp.float32)
    second_sum = lax.psum_scatter(
        jnp.concatenate([t.astype(jnp.bfloat16) for t in scatter_cols[4:]], axis=1),
        "seq",
        scatter_dimension=0,
        tiled=True,
    ).astype(jnp.float32)
    out_weight_grad = first_sum[:, :head_cols].T
    gate_weight_grad = first_sum[:, head_cols : head_cols + hidden]
    up_weight_grad = first_sum[:, head_cols + hidden : head_cols + 2 * hidden]
    down_weight_grad = first_sum[:, head_cols + 2 * hidden :].T
    query_weight_grad = second_sum[:, :head_cols]
    key_weight_grad = second_sum[:, head_cols : 2 * head_cols]
    value_weight_grad = second_sum[:, 2 * head_cols : 3 * head_cols]
    forget_weight_grad = second_sum[:, 3 * head_cols : 3 * head_cols + local_heads]
    attn_gain_grad, ffn_gain_grad, forget_bias_grad = lax.psum(
        (gain_one, gain_two, jnp.sum(grad_logit, axis=0)), "seq"
    )
    return (
        layer_out,
        tokens_grad,
        attn_gain_grad,
        query_weight_grad,
        key_weight_grad,
        value_weight_grad,
        forget_weight_grad,
        forget_bias_grad,
        out_weight_grad,
        ffn_gain_grad,
        gate_weight_grad,
        up_weight_grad,
        down_weight_grad,
    )


def body(*args):
    fits = kernels_fit(args[0], args[6], args[9])
    return (kernel_body if fits else plain_body)(*args)


def solution(mesh):
    return jax.shard_map(
        body,
        mesh=mesh,
        in_specs=(
            P("seq", None),
            P(),
            P("seq", "head"),
            P("seq", "head"),
            P("seq", "head"),
            P("seq", "head"),
            P("head"),
            P("head", "seq"),
            P(),
            P("seq", "head"),
            P("seq", "head"),
            P("head", "seq"),
            P(),
            P("seq", None),
        ),
        out_specs=(
            P("seq", None),
            P("seq", None),
            P(),
            P("seq", "head"),
            P("seq", "head"),
            P("seq", "head"),
            P("seq", "head"),
            P("head"),
            P("head", "seq"),
            P(),
            P("seq", "head"),
            P("seq", "head"),
            P("head", "seq"),
        ),
        check_vma=False,
    )
```

profile of v0, /device:TPU:0, one launch (start us, length us, event | category | flops | bytes accessed | tf_op | source)
XLA Modules:
  0.0 273.3 jit_solution(4046642728529381390)
XLA Ops:
  0.7 266.6 %shard_map.237 = (bf16[256,1536]{1,0:T(8,128)(2,1)}, bf16[256,1536]{1,0:T(8,128)(2,1)}, f32[8,384]{1,0:T(8,128)}, f32[2,8,128]{2,1,0:T(8,128)}, bf16[2,192,512]{...) custom-call(bf16[256,1536]{1,0:T(8,128)(2,1)} %tokens.1, ...), custom_call_target="tpu_custom_call" | custom-call | tf_op jit(solution)/shard_map/pallas_call | solution.py:1525
  267.3 4.5 %shard_map.238 = (bf16[256,1536]{1,0:T(8,128)(2,1)}, bf16[256,1536]{1,0:T(8,128)(2,1)}, f32[1536]{0:T(1024)}, f32[192,384]{1,0:T(8,128)}, f32[192,384]{1,0:T(8,1...) custom-call(bf16[256,1536]{1,0:T(8,128)(2,1)} %get-tuple-element.34., ...), custom_call_target="tpu_custom_call" | custom-call | tf_op jit(solution)/shard_map/pallas_call | solution.py:1565
  271.8 1.3 slice_reduce_fusion
where the time goes:
time: 278 us; the launch traced here: 273 us
  Pallas kernels  271 us (97%)
    pallas_call x1, Pallas kernels, kernel_body(): pl.pallas_call(layer_kernel, out_shape=shapes_of(outs), in_specs=[HBM] *...  267 us

commit v1 on v0

--- a/solution.py
+++ b/solution.py
@@ -1110,18 +1110,19 @@
         grad_attn[y, rows_of(z * chunk + k * sub, sub), :] = grad_middle[k].astype(BF16)
         attn_nets[k].start()
     to_out = slice(2 * hidden, 3 * hidden)
-    out_sends = [lower_of(part_out, out_low, 0, to_out), None]
     attn_nets[0].forward()
-    out_sends[1] = lower_of(part_out, out_low, 1, to_out)
     every = places.every((1, places.all), 1)
     own_pos = [
         places.position(places.own(late) + lax.broadcasted_iota(jnp.int32, (part, 1), 0))
         for late in range(2)
     ]
     attn_nets[1].forward()
+    out_sends = [lower_of(part_out, out_low, k, to_out) for k in range(2)]
     attn_nets[0].finish()
     query_net.finish()
     attn_nets[1].finish()
+    for k in range(2):
+        upper_of(out_sends[k], part_out, out_low, k, outs)
 
     lane = lax.broadcasted_iota(jnp.int32, (part, LANES), 1)
     for late in range(2):
@@ -1146,8 +1147,8 @@
         left = grad_attn[:, :, cols].reshape(2 * part, tile)
         early_sum[cols, :] = dot_tn(left, mixed[...]).astype(BF16)
     early_net.start()
-    for k in range(2):
-        upper_of(out_sends[k], part_out, out_low, k, outs)
+    for out in outs:
+        out.middle()
     ffn_net.second()
 
     lane = lax.broadcasted_iota(jnp.int32, (LANES, LANES), 1)
@@ -1183,8 +1184,7 @@
             grad_net.forward()
             stat_net.forward()
         if block == 1:
-            for out in outs:
-                out.middle()
+            pass
             early_net.second()
 
     starts = doc_starts(every, doc_ref)

time: 278 us -> 279 us (level)
  no operation moved by 1% of the time
where the time goes in v1:
time: 279 us; the launch traced here: 273 us
  Pallas kernels  271 us (97%)
    pallas_call x1, Pallas kernels, kernel_body(): pl.pallas_call(layer_kernel, out_shape=shapes_of(outs), in_specs=[HBM] *...  267 us

profile of v1, /device:TPU:0, one launch (start us, length us, event | category | flops | bytes accessed | tf_op | source)
XLA Modules:
  0.0 273.4 jit_solution(6137965472496578804)
XLA Ops:
  0.7 266.7 %shard_map.237 = (bf16[256,1536]{1,0:T(8,128)(2,1)}, bf16[256,1536]{1,0:T(8,128)(2,1)}, f32[8,384]{1,0:T(8,128)}, f32[2,8,128]{2,1,0:T(8,128)}, bf16[2,192,512]{...) custom-call(bf16[256,1536]{1,0:T(8,128)(2,1)} %tokens.1, ...), custom_call_target="tpu_custom_call" | custom-call | tf_op jit(solution)/shard_map/pallas_call | solution.py:1525
  267.4 4.5 %shard_map.238 = (bf16[256,1536]{1,0:T(8,128)(2,1)}, bf16[256,1536]{1,0:T(8,128)(2,1)}, f32[1536]{0:T(1024)}, f32[192,384]{1,0:T(8,128)}, f32[192,384]{1,0:T(8,1...) custom-call(bf16[256,1536]{1,0:T(8,128)(2,1)} %get-tuple-element.34., ...), custom_call_target="tpu_custom_call" | custom-call | tf_op jit(solution)/shard_map/pallas_call | solution.py:1565
  271.9 1.3 slice_reduce_fusion
